TPU v7x, 512 devices: a whole 4x4x16 slice. The times are simulated.
512 devices in a mesh: bulk: 32 (over z, y_lo), group: 16 (over y_hi, x, core).
Axes of the slice: x: 4, y: 4 (y_hi: 2, y_lo: 2; y = y_hi * 2 + y_lo), z: 16, core: 2. Of those that a mesh axis runs over, the one named last changes fastest.
Arguments:
- snapshots: bfloat16 [3145728, 128], P(('bulk', 'group'))
- owned_rows: int32 [512], P(('bulk', 'group')), may hold values from 3072 to 6144, as said below
- iface_lists: int32 [512, 4, 512], P(('bulk', 'group')), may hold values from 0 to 6143, as said below
- block_columns: int32 [49152, 9], P(('bulk', 'group')), may hold values from 0 to 127, as said below
- block_types: int32 [49152, 9], P(('bulk', 'group')), may hold values from 0 to 15
- block_scales: float32 [49152, 9], P(('bulk', 'group')), may hold values from 0.2 to 0.8
- mass_table: bfloat16 [16, 64, 64], replicated
- sketch_matrix: bfloat16 [128, 256], replicated, may hold values from -0.5 to 0.5
Outputs:
- projected: bfloat16 [3145728, 256], P(('bulk', 'group'))
- sketch: float32 [128, 256], replicated
Inputs may be any that keep to these rules, and one draw needn't show every extreme that they name: Partition p owns its first owned_rows[p] rows; the rest of its 6144 rows are padding. Some partition owns all 6144. iface_lists[p, d] lists, with possible repeats, local owned rows of partition p (each below owned_rows[p]) for its neighbour d: 0 and 1 the lower and upper one along bulk, 2 and 3 the lower and upper one along group. `block_columns`: block row i of partition p names own block j < 96 or ghost block 96 + j; every ghost block is named by some block row of every partition.
All inputs are finite; a program needn't handle non-finite values.
Results may differ from a plain program's by a relative error of at most 0.0041.
The roundings to bfloat16 on the way count: a program that leaves them out, or rounds other values in their place, can miss the bound.
Values may be sent and summed in bfloat16 or wider, within the bound.
A program may use at most 64 MiB of HBM per device.

v0:
```python
import jax
import jax.numpy as jnp
from jax import lax
from jax.sharding import PartitionSpec as P


def extended(cells, sides, width, closed):
    for axis, dim in sides:
        count = lax.axis_size(axis)
        ends = count if closed else count - 1
        head = lax.slice_in_dim(cells, 0, width, axis=dim)
        tail = lax.slice_in_dim(cells, cells.shape[dim] - width, cells.shape[dim], axis=dim)
        cells = jnp.concatenate(
            [
                lax.ppermute(tail, axis, [(i, (i + 1) % count) for i in range(ends)]),
                cells,
                lax.ppermute(head, axis, [((i + 1) % count, i) for i in range(ends)]),
            ],
            axis=dim,
        )
    return cells


def on_device(
    snapshots,
    owned_rows,
    iface_lists,
    block_columns,
    block_types,
    block_scales,
    mass_table,
    sketch_matrix,
):
    row_count, snap_count = snapshots.shape
    block_size = mass_table.shape[1]
    face_count = iface_lists.shape[2]
    owned_mask = jnp.arange(row_count) < owned_rows[0]
    panel = jnp.where(owned_mask[:, None], snapshots, jnp.zeros((), snapshots.dtype))
    outgoing = panel[iface_lists[0].reshape(-1)].reshape(4, face_count, snap_count)
    bulk_pair = jnp.concatenate([outgoing[0], outgoing[1]], axis=0)
    bulk_padded = extended(bulk_pair, (("bulk", 0),), face_count, False)
    group_pair = jnp.concatenate([outgoing[2], outgoing[3]], axis=0)
    group_padded = extended(group_pair, (("group", 0),), face_count, True)
    ghosts = jnp.concatenate(
        [
            bulk_padded[:face_count],
            bulk_padded[3 * face_count :],
            group_padded[:face_count],
            group_padded[3 * face_count :],
        ],
        axis=0,
    )
    node_blocks = jnp.concatenate([panel, ghosts], axis=0).reshape(-1, block_size, snap_count)

    def add_entry(accumulated, entry):
        column_ids, type_ids, jacobians = entry
        ref_tiles = mass_table[type_ids]
        gathered = node_blocks[column_ids]
        term_value = jnp.einsum(
            "bij,bjs->bis", ref_tiles, gathered, preferred_element_type=jnp.float32
        )
        return (accumulated + jacobians[:, None, None] * term_value, None)

    start_value = jnp.zeros((row_count // block_size, block_size, snap_count), jnp.float32)
    accumulated, _ = lax.scan(
        add_entry, start_value, (block_columns.T, block_types.T, block_scales.T)
    )
    weighted = jnp.where(
        owned_mask[:, None], accumulated.reshape(row_count, snap_count), jnp.zeros((), jnp.float32)
    ).astype(jnp.bfloat16)
    projected = jnp.dot(weighted, sketch_matrix, preferred_element_type=jnp.float32).astype(
        jnp.bfloat16
    )
    local_gram = jnp.einsum("ns,nt->st", panel, weighted, preferred_element_type=jnp.float32)
    sketch_f32 = sketch_matrix.astype(jnp.float32)
    local_sketch = jnp.dot(local_gram, sketch_f32, precision=lax.Precision.HIGHEST)
    sketch = lax.psum(local_sketch, ("bulk", "group")) / row_count
    return (projected, sketch)


def solution(mesh):
    return jax.shard_map(
        on_device,
        mesh=mesh,
        in_specs=(
            P(("bulk", "group"), None),
            P(("bulk", "group")),
            P(("bulk", "group"), None, None),
            P(("bulk", "group"), None),
            P(("bulk", "group"), None),
            P(("bulk", "group"), None),
            P(),
            P(),
        ),
        out_specs=(P(("bulk", "group"), None), P()),
        check_vma=False,
    )
```

profile of v0, /device:TPU:1, one launch (start us, length us, event | category | flops | bytes accessed | tf_op | source)
XLA Modules:
  0.0 588.0 jit_solution(15095892241410316989)
XLA Ops:
  8.6 5.3 constant_dynamic-update-slice_fusion.4
  13.9 1.2 copy-done.2
  15.1 6.2 %gather_fusion.2 = bf16[2048,128]{1,0:T(8,128)(2,1)S(1)} fusion(bf16[6144,128]{1,0:T(8,128)(2,1)S(1)} %get-tuple-element.79, s32[2048]{0:T(1024)S(1)} %broadcast_clamp_fusion), kind=kCustom, calls=%fused_computation.2 | custom fusion | bytes 1056768 | tf_op jit(solution)/shard_map/gather | solution.py:39
  21.3 4.2 collective-permute-start
  25.5 1.3 collective-permute-start.1
  26.8 6.0 %collective-permute-start.3 = (bf16[512,128]{1,0:T(8,128)(2,1)S(1)}, bf16[512,128]{1,0:T(8,128)(2,1)S(1)}, u32[]{:S(2)}, u32[]{:S(2)}) collective-permute-start(bf16[512,128]{1,0:T(8,128)(2,1)S(1)} %get-tuple-element.82), channel_id=1, source_target_pairs={{1,0},{2,1},{3,2},{4,3},{5,4},{6,5},{7,6},{8,7},{9,8},{10,9},{11,1... | collective-permute-start | bytes 393224 | tf_op jit(solution)/shard_map/ppermute | solution.py:17
  32.8 1.9 collective-permute-start.2
  38.0 77.8 %while.11 = (s32[]{:T(128)}, f32[96,64,128]{2,1,0:T(8,128)}, f32[9,96]{1,0:T(8,128)}, s32[9,96]{1,0:T(8,128)}, bf16[16,64,64]{2,1,0:T(8,128)(2,1)S(1)}, /*index=...) while((s32[]{:T(128)}, f32[96,64,128]{2,1,0:T(8,128)}, ...), condition=%wide.region_1.2_spmd.clone, body=%wide.region_0.1_spmd.clone.sunk | while | flops 103025216 | bytes 13381879 | solution.py:65
  38.7 0.7 fusion.23
  39.5 2.4 gather_fusion.1
  41.9 0.8 gather_fusion
  42.8 2.2 select_add_fusion.2
  45.7 0.7 fusion.23
  46.4 2.4 gather_fusion.1
  48.9 0.8 gather_fusion
  49.7 4.1 select_add_fusion.2
  54.5 0.7 fusion.23
  55.3 2.4 gather_fusion.1
  57.7 0.8 gather_fusion
  58.6 4.1 select_add_fusion.2
  63.4 0.7 fusion.23
  64.1 2.4 gather_fusion.1
  66.6 0.8 gather_fusion
  67.4 4.1 select_add_fusion.2
  72.2 0.7 fusion.23
  73.0 2.4 gather_fusion.1
  75.4 0.8 gather_fusion
  76.3 4.1 select_add_fusion.2
  81.1 0.7 fusion.23
  81.8 2.4 gather_fusion.1
  84.3 0.8 gather_fusion
  85.1 4.1 select_add_fusion.2
  90.0 0.7 fusion.23
  90.7 2.4 gather_fusion.1
  93.1 0.8 gather_fusion
  94.0 4.1 select_add_fusion.2
  98.8 0.7 fusion.23
  99.5 2.4 gather_fusion.1
  102.0 0.8 gather_fusion
  102.8 4.1 select_add_fusion.2
  108.4 2.4 gather_fusion.1
  110.8 0.8 gather_fusion
  111.7 4.1 select_add_fusion.2
  115.8 4.8 fusion.5
  121.2 0.9 fusion.8
  122.1 2.6 convolution_convert_fusion
  124.8 454.9 %all-reduce.2.cloned.1.call-done = f32[128,256]{1,0:T(8,128)} async-done(((f32[128,256]{1,0:T(8,128)}), f32[128,256]{1,0:T(8,128)}) %all-reduce.2.cloned.1.call-update) | async-done | bytes 131088 | tf_op jit(solution)/shard_map/psum | solution.py:77
  579.6 1.6 broadcast_multiply_fusion
  (52 shorter events, 11.7 us)
Async XLA Ops:
  7.2 114.1 %copy-start = (bf16[128,256]{1,0:T(8,128)(2,1)S(1)}, bf16[128,256]{1,0:T(8,128)(2,1)}, u32[]{:S(2)}) copy-start(bf16[128,256]{1,0:T(8,128)(2,1)} %param.17) | copy-start | bytes 196612
  7.2 572.4 %all-reduce.2.cloned.1.call-start = ((), (), s32[]{:S(2)}) async-start(), calls=%async_computation | async-start | bytes 262144 | tf_op jit(solution)/shard_map/psum | solution.py:77
  13.9 1.2 copy-start.2
  21.3 16.8 %copy-start.1 = (bf16[16,64,64]{2,1,0:T(8,128)(2,1)S(1)}, bf16[16,64,64]{2,1,0:T(8,128)(2,1)}, u32[]{:S(2)}) copy-start(bf16[16,64,64]{2,1,0:T(8,128)(2,1)} %param.16) | copy-start | bytes 393220
  21.3 13.5 %collective-permute-start = (bf16[512,128]{1,0:T(8,128)(2,1)S(1)}, bf16[512,128]{1,0:T(8,128)(2,1)S(1)}, u32[]{:S(2)}, u32[]{:S(2)}) collective-permute-start(bf16[512,128]{1,0:T(8,128)(2,1)S(1)} %get-tuple-element.85), channel_id=1, source_target_pairs={{0,16},{16,32},{32,48},{48,64},{64,80},{80,96},{96,112},{112,128},... | collective-permute-start | bytes 393224 | tf_op jit(solution)/shard_map/ppermute | solution.py:15
  25.5 10.0 %collective-permute-start.1 = (bf16[512,128]{1,0:T(8,128)(2,1)S(1)}, bf16[512,128]{1,0:T(8,128)(2,1)S(1)}, u32[]{:S(2)}, u32[]{:S(2)}) collective-permute-start(bf16[512,128]{1,0:T(8,128)(2,1)S(1)} %get-tuple-element.84), channel_id=1, source_target_pairs={{16,0},{32,16},{48,32},{64,48},{80,64},{96,80},{112,96},{128,112},... | collective-permute-start | bytes 393224 | tf_op jit(solution)/shard_map/ppermute | solution.py:17
  26.8 10.6 %collective-permute-start.3 = (bf16[512,128]{1,0:T(8,128)(2,1)S(1)}, bf16[512,128]{1,0:T(8,128)(2,1)S(1)}, u32[]{:S(2)}, u32[]{:S(2)}) collective-permute-start(bf16[512,128]{1,0:T(8,128)(2,1)S(1)} %get-tuple-element.82), channel_id=1, source_target_pairs={{1,0},{2,1},{3,2},{4,3},{5,4},{6,5},{7,6},{8,7},{9,8},{10,9},{11,1... | collective-permute-start | bytes 393224 | tf_op jit(solution)/shard_map/ppermute | solution.py:17
  32.8 3.9 collective-permute-start.2
  115.8 4.8 copy-start.3
Sparse Core Ops, SparseCore 0:
  122.3 457.3 all-reduce.1
where the time goes:
time: 590 us; the launch traced here: 588 us
  waiting for transfers between devices  455 us (77%)
  local copies, waits for them, and re-layouts  46.6 us (8%)
  matrix products  39.3 us (7%)
  other arithmetic  18.2 us (3%)
  between operations  14.8 us (3%)
  starting transfers between devices  13.5 us (2%)
    psum x1, waiting for transfers between devices, on_device(): sketch = lax.psum(local_sketch, ('bulk', 'group')) / row_count  455 us
    dot_general x9, matrix products, add_entry(): jnp.einsum('bij,bjs->bis', ref_tiles, gathered, preferred_element_type=jn...  35.2 us
    gather x9, local copies, waits for them, and re-layouts, add_entry(): gathered = node_blocks[column_ids]  22 us
  transfers between devices with their start and end apart: 5, of which 2 were waited for; matrix products, arithmetic and copies ran while one was open for 1% of the time, Pallas kernels for 0%

commit v1 on v0

v1 whole, which is shorter than its diff:
```python
import functools

import jax
import jax.numpy as jnp
from jax import lax
from jax.experimental import pallas as pl
from jax.experimental.pallas import tpu as pltpu
from jax.sharding import PartitionSpec as P

MESH = pl.DeviceIdType.MESH
NEAR = 2
MIB = 1 << 20


def rows_kernel(
    bulk_n, group_n, lists, snap_hbm, ghosts, snap, wide, picked, packed, load_sem, send_sem, recv_sem
):
    row_count = snap.shape[0]
    faces = packed.shape[1]
    b, g = lax.axis_index("bulk"), lax.axis_index("group")
    above, below = lax.rem(b + 1, bulk_n), lax.rem(b + bulk_n - 1, bulk_n)
    right, left = lax.rem(g + 1, group_n), lax.rem(g + group_n - 1, group_n)
    plan = ((1, (above, g)), (0, (below, g)), (3, (b, right)), (2, (b, left)))

    load = pltpu.make_async_copy(snap_hbm, snap, load_sem)
    load.start()
    barrier = pltpu.get_barrier_semaphore()
    for _, peer in plan:
        pl.semaphore_signal(barrier, inc=1, device_id=peer, device_id_type=MESH)
    load.wait()
    step = 256

    def widen(i, carry):
        rows = pl.ds(pl.multiple_of(i * step, step), step)
        wide[rows, :] = snap[rows, :].astype(jnp.float32)
        return carry

    lax.fori_loop(0, row_count // step, widen, 0)
    pl.semaphore_wait(barrier, len(plan))

    copies = []
    for slot, (which, peer) in enumerate(plan):

        def pick(i, carry):
            for u in range(16):
                r = i * 16 + u
                picked[pl.ds(r, 1), :] = wide[pl.ds(lists[0, which, r], 1), :]
            return carry

        lax.fori_loop(0, faces // 16, pick, 0)
        packed[slot] = picked[...].astype(jnp.bfloat16)
        copy = pltpu.make_async_remote_copy(
            src_ref=packed.at[slot],
            dst_ref=ghosts.at[slot],
            send_sem=send_sem.at[slot],
            recv_sem=recv_sem.at[slot],
            device_id=peer,
            device_id_type=MESH,
        )
        copy.start()
        copies.append(copy)
    for copy in copies:
        copy.wait()


def exchanged(snapshots, iface_lists, bulk_n, group_n):
    rows, snaps = snapshots.shape
    faces = iface_lists.shape[2]
    return pl.pallas_call(
        functools.partial(rows_kernel, bulk_n, group_n),
        out_shape=jax.ShapeDtypeStruct((4, faces, snaps), jnp.bfloat16),
        in_specs=[pl.BlockSpec(memory_space=pltpu.SMEM), pl.BlockSpec(memory_space=pl.ANY)],
        out_specs=pl.BlockSpec(memory_space=pl.ANY),
        scratch_shapes=[
            pltpu.VMEM((rows, snaps), jnp.bfloat16),
            pltpu.VMEM((rows, snaps), jnp.float32),
            pltpu.VMEM((faces, snaps), jnp.float32),
            pltpu.VMEM((4, faces, snaps), jnp.bfloat16),
            pltpu.SemaphoreType.DMA,
            pltpu.SemaphoreType.DMA((4,)),
            pltpu.SemaphoreType.DMA((4,)),
        ],
        compiler_params=pltpu.CompilerParams(
            collective_id=0, has_side_effects=True, vmem_limit_bytes=24 * MIB
        ),
        name="ghost_rows",
    )(iface_lists, snapshots)


def mass_kernel(
    edges, entries, owned, columns, types, scales, snap, ghosts, table, test,
    projected, gram, cols, pairs, weighted, total,
):
    step, steps = pl.program_id(0), pl.num_programs(0)
    own, block, snaps = snap.shape
    outer = ghosts.shape[0]
    per_step = projected.shape[0] // block
    lane = lax.broadcasted_iota(jnp.int32, (1, 2 * block), 1) < block
    line = lax.broadcasted_iota(jnp.int32, (block, snaps), 0)
    count = owned[0]

    @pl.when(step == 0)
    def _():
        b = lax.axis_index("bulk")
        total[...] = jnp.zeros_like(total)
        for t in range(table.shape[0]):
            both = table[t].astype(jnp.float32)
            pairs[t] = jnp.concatenate([both, both], axis=1)

        def own_blocks(i, carry):
            keep = line + i * block < count
            cols[i] = jnp.where(keep, snap[i].astype(jnp.float32), 0.0).astype(jnp.bfloat16)
            return carry

        def ghost_blocks(i, carry):
            side = i // (outer // 4)
            gone = ((side == 0) & (b == 0)) | ((side == 1) & (b == edges - 1))
            value = ghosts[i].astype(jnp.float32)
            keep = line < jnp.where(gone, 0, block)
            cols[own + i] = jnp.where(keep, value, 0.0).astype(jnp.bfloat16)
            return carry

        lax.fori_loop(0, own, own_blocks, 0)
        lax.fori_loop(0, outer, ghost_blocks, 0)

    for u in range(per_step):
        r = step * per_step + u
        tiles = []
        for k in range(0, entries - 1, 2):
            one, two = pairs[types[k, r]], pairs[types[k + 1, r]]
            factor = jnp.where(lane, scales[k, r], scales[k + 1, r])
            tiles.append((jnp.where(lane, one, two) * factor).astype(jnp.bfloat16))
        if entries % 2:
            last = pairs[types[entries - 1, r]][:, :block] * scales[entries - 1, r]
            tiles.append(last.astype(jnp.bfloat16))
        stacked = jnp.concatenate([cols[columns[k, r]] for k in range(entries)], axis=0)
        value = jnp.dot(
            jnp.concatenate(tiles, axis=1), stacked, preferred_element_type=jnp.float32
        )
        keep = line + r * block < count
        weighted[u * block : (u + 1) * block, :] = jnp.where(keep, value, 0.0).astype(jnp.bfloat16)

    here = weighted[...]
    projected[...] = jnp.dot(here, test[...], preferred_element_type=jnp.float32).astype(jnp.bfloat16)
    mine = snap[pl.ds(step * per_step, per_step)].reshape(per_step * block, snaps)
    total[...] += lax.dot_general(
        mine, here, (((0,), (0,)), ((), ())), preferred_element_type=jnp.float32
    )

    @pl.when(step == steps - 1)
    def _():
        parts, height = gram.shape[0], gram.shape[1]
        for p in range(parts):
            gram[p] = total[p * height : (p + 1) * height, :]


def mass_product(owned, columns, types, scales, snapshots, ghosts, table, test, edges, parts):
    rows, snaps = snapshots.shape
    kinds, block, _ = table.shape
    own, outer = rows // block, ghosts.shape[0] * ghosts.shape[1] // block
    entries = columns.shape[1]
    width = test.shape[1]
    per_step = 8
    whole = lambda shape: pl.BlockSpec(shape, lambda i: (0,) * len(shape))
    scalar = pl.BlockSpec(memory_space=pltpu.SMEM)
    return pl.pallas_call(
        functools.partial(mass_kernel, edges, entries),
        grid=(own // per_step,),
        out_shape=(
            jax.ShapeDtypeStruct((rows, width), jnp.bfloat16),
            jax.ShapeDtypeStruct((parts, snaps // parts, snaps), jnp.float32),
        ),
        in_specs=[
            scalar, scalar, scalar, scalar,
            whole((own, block, snaps)),
            whole((outer, block, snaps)),
            whole((kinds, block, block)),
            whole((snaps, width)),
        ],
        out_specs=(
            pl.BlockSpec((per_step * block, width), lambda i: (i, 0)),
            whole((parts, snaps // parts, snaps)),
        ),
        scratch_shapes=[
            pltpu.VMEM((own + outer, block, snaps), jnp.bfloat16),
            pltpu.VMEM((kinds, block, 2 * block), jnp.float32),
            pltpu.VMEM((per_step * block, snaps), jnp.bfloat16),
            pltpu.VMEM((snaps, snaps), jnp.float32),
        ],
        compiler_params=pltpu.CompilerParams(vmem_limit_bytes=32 * MIB),
        name="mass_product",
    )(
        owned, columns.T, types.T, scales.T,
        snapshots.reshape(own, block, snaps),
        ghosts.reshape(outer, block, snaps),
        table, test,
    )


def total_kernel(
    bulk_n, group_n, divisor, gram, test, sketch,
    near, far, whole, full, send_a, recv_a, send_b, recv_b, send_c, recv_c,
):
    parts, height, snaps = gram.shape
    depth = bulk_n // NEAR
    b, g = lax.axis_index("bulk"), lax.axis_index("group")
    z, q = b // NEAR, lax.rem(b, NEAR) * group_n + g

    def in_plane(d):
        other = lax.rem(q + d, parts)
        return other, (z * NEAR + other // group_n, lax.rem(other, group_n))

    def along_z(d):
        other = lax.rem(z + d, depth)
        return other, (other * NEAR + lax.rem(b, NEAR), g)

    barrier = pltpu.get_barrier_semaphore()

    def greet(where):
        def body(d, carry):
            _, peer = where(d)
            pl.semaphore_signal(barrier, inc=1, device_id=peer, device_id_type=MESH)
            return carry
        return body

    lax.fori_loop(1, parts, greet(in_plane), 0)
    lax.fori_loop(1, depth, greet(along_z), 0)
    near[pl.ds(q, 1)] = gram[pl.ds(q, 1)]
    pl.semaphore_wait(barrier, parts + depth - 2)

    def scatter(d):
        other, peer = in_plane(d)
        return pltpu.make_async_remote_copy(
            src_ref=gram.at[other], dst_ref=near.at[q], send_sem=send_a.at[d], recv_sem=recv_a.at[d],
            device_id=peer, device_id_type=MESH,
        )

    def spread(d):
        _, peer = along_z(d)
        return pltpu.make_async_remote_copy(
            src_ref=far.at[z], dst_ref=far.at[z], send_sem=send_b.at[d], recv_sem=recv_b.at[d],
            device_id=peer, device_id_type=MESH,
        )

    def gather(d):
        _, peer = in_plane(d)
        return pltpu.make_async_remote_copy(
            src_ref=whole.at[q], dst_ref=whole.at[q], send_sem=send_c.at[d], recv_sem=recv_c.at[d],
            device_id=peer, device_id_type=MESH,
        )

    def start(make):
        def body(d, carry):
            make(d).start()
            return carry
        return body

    def arrive(make):
        def body(d, carry):
            make(d).wait_recv()
            return carry
        return body

    def leave(make):
        def body(d, carry):
            make(d).wait_send()
            return carry
        return body

    lax.fori_loop(1, parts, start(scatter), 0)
    lax.fori_loop(1, parts, arrive(scatter), 0)
    far[pl.ds(z, 1)] = jnp.sum(near[...], axis=0, keepdims=True)
    lax.fori_loop(1, depth, start(spread), 0)
    lax.fori_loop(1, depth, arrive(spread), 0)
    whole[pl.ds(q, 1)] = jnp.sum(far[...], axis=0, keepdims=True)
    lax.fori_loop(1, parts, start(gather), 0)
    lax.fori_loop(1, parts, arrive(gather), 0)
    for p in range(parts):
        full[p * height : (p + 1) * height, :] = whole[p]
    sketch[...] = (
        jnp.dot(
            full[...], test[...].astype(jnp.float32),
            precision=lax.Precision.HIGHEST, preferred_element_type=jnp.float32,
        )
        / divisor
    )
    lax.fori_loop(1, parts, leave(scatter), 0)
    lax.fori_loop(1, depth, leave(spread), 0)
    lax.fori_loop(1, parts, leave(gather), 0)


def summed_sketch(gram, test, divisor, bulk_n, group_n):
    parts, height, snaps = gram.shape
    depth = bulk_n // NEAR
    width = test.shape[1]
    vmem = pl.BlockSpec(memory_space=pltpu.VMEM)
    return pl.pallas_call(
        functools.partial(total_kernel, bulk_n, group_n, divisor),
        out_shape=jax.ShapeDtypeStruct((snaps, width), jnp.float32),
        in_specs=[vmem, vmem],
        out_specs=vmem,
        scratch_shapes=[
            pltpu.VMEM((parts, height, snaps), jnp.float32),
            pltpu.VMEM((depth, height, snaps), jnp.float32),
            pltpu.VMEM((parts, height, snaps), jnp.float32),
            pltpu.VMEM((snaps, snaps), jnp.float32),
            pltpu.SemaphoreType.DMA((parts,)),
            pltpu.SemaphoreType.DMA((parts,)),
            pltpu.SemaphoreType.DMA((depth,)),
            pltpu.SemaphoreType.DMA((depth,)),
            pltpu.SemaphoreType.DMA((parts,)),
            pltpu.SemaphoreType.DMA((parts,)),
        ],
        compiler_params=pltpu.CompilerParams(
            collective_id=1, has_side_effects=True, vmem_limit_bytes=16 * MIB
        ),
        name="gram_total",
    )(gram, test)


def on_device(
    bulk_n, group_n,
    snapshots, owned_rows, iface_lists, block_columns, block_types, block_scales, mass_table, sketch_matrix,
):
    ghosts = exchanged(snapshots, iface_lists, bulk_n, group_n)
    projected, gram = mass_product(
        owned_rows, block_columns, block_types, block_scales,
        snapshots, ghosts, mass_table, sketch_matrix, bulk_n, NEAR * group_n,
    )
    sketch = summed_sketch(gram, sketch_matrix, snapshots.shape[0], bulk_n, group_n)
    return projected, sketch


def solution(mesh):
    return jax.shard_map(
        functools.partial(on_device, mesh.shape["bulk"], mesh.shape["group"]),
        mesh=mesh,
        in_specs=(
            P(("bulk", "group"), None),
            P(("bulk", "group")),
            P(("bulk", "group"), None, None),
            P(("bulk", "group"), None),
            P(("bulk", "group"), None),
            P(("bulk", "group"), None),
            P(),
            P(),
        ),
        out_specs=(P(("bulk", "group"), None), P()),
        check_vma=False,
    )
```

time: 590 us -> 69 us (0.12)
  waiting for transfers between devices: 455 us -> 0 us
  Pallas kernels: 0 us -> 60.7 us
  local copies, waits for them, and re-layouts: 46.6 us -> 6.63 us
  matrix products: 39.3 us -> 0 us
  other arithmetic: 18.2 us -> 0 us
  starting transfers between devices: 13.5 us -> 0 us
  between operations: 14.8 us -> 1.32 us
    psum x1 -> x0, waiting for transfers between devices: 455 us -> none  [on_device(): sketch = lax.psum(local_sketch, ('bulk', 'group')) / row_count]
    pallas_call x0 -> x3, Pallas kernels: none -> 60.7 us  [the longest x1 27.1 us: summed_sketch(): pl.pallas_call(functools.partial(total_kernel, bulk_n, group_n, divisor),...]
    dot_general x12 -> x0, matrix products: 39.3 us -> none  [the longest x9 35.2 us: add_entry(): jnp.einsum('bij,bjs->bis', ref_tiles, gathered, preferred_element_type=jn...]
    gather x19 -> x0, local copies, waits for them, and re-layouts: 35.8 us -> none  [the longest x9 22 us: add_entry(): gathered = node_blocks[column_ids]]
    ppermute x4 -> x0, starting transfers between devices: 13.4 us -> none  [the longest x2 7.34 us: extended(): lax.ppermute(head, axis, [((i + 1) % count, i) for i in range(ends)])]
    select_n x10 -> x0, other arithmetic: 6.4 us -> none  [the longest x9 6.39 us: add_entry(): ref_tiles = mass_table[type_ids]]
    mul x9 -> x0, local copies, waits for them, and re-layouts: 6.22 us -> none  [add_entry(): return (accumulated + jacobians[:, None, None] * term_value, None)]
  transfers between devices with their start and end apart: 5 -> 0, of which waited for: 2 -> 0; matrix products, arithmetic and copies ran while one was open for 1% -> 0% of each run, Pallas kernels for 0% -> 0%
where the time goes in v1:
time: 69 us; the launch traced here: 68.6 us
  Pallas kernels  60.7 us (88%)
  local copies, waits for them, and re-layouts  6.63 us (10%)
  between operations  1.32 us (2%)
    pallas_call x1, Pallas kernels, summed_sketch(): pl.pallas_call(functools.partial(total_kernel, bulk_n, group_n, divisor),...  27.1 us
    pallas_call x1, Pallas kernels, exchanged(): pl.pallas_call(functools.partial(rows_kernel, bulk_n, group_n), out_shape...  22.6 us
    pallas_call x1, Pallas kernels, mass_product(): pl.pallas_call(functools.partial(mass_kernel, edges, entries), grid=(own...  10.9 us
    unnamed x17, local copies, waits for them, and re-layouts  6.63 us

profile of v1, /device:TPU:1, one launch (start us, length us, event | category | flops | bytes accessed | tf_op | source)
XLA Modules:
  0.0 68.6 jit_solution(13768018112113250183)
XLA Ops:
  1.3 0.0 copy-start
  1.3 1.4 %copy-done = bf16[6144,128]{1,0:T(8,128)(2,1)S(1)} copy-done((bf16[6144,128]{1,0:T(8,128)(2,1)S(1)}, bf16[6144,128]{1,0:T(8,128)(2,1)}, u32[]{:S(2)}) %copy-start) | copy-done | bytes 1572888
  2.7 0.0 copy-start.4
  2.7 0.7 %copy-done.4 = s32[1,4,512]{2,1,0:T(4,128)S(1)} copy-done((s32[1,4,512]{2,1,0:T(4,128)S(1)}, s32[1,4,512]{2,1,0:T(4,128)}, u32[]{:S(2)}) %copy-start.4) | copy-done | bytes 8216
  3.4 0.0 copy-start.1
  3.4 22.6 %ghost_rows.1 = bf16[4,512,128]{2,1,0:T(8,128)(2,1)S(1)} custom-call(s32[1,4,512]{2,1,0:T(4,128)S(1)} %copy-done.4, bf16[6144,128]{1,0:T(8,128)(2,1)S(1)} %copy-done), custom_call_target="tpu_custom_call" | custom-call | tf_op jit(solution)/shard_map/ghost_rows/pallas_call | solution.py:69
  26.0 0.0 copy-done.1
  26.0 0.0 copy-start.2
  26.0 0.8 %copy-done.2 = bf16[128,256]{1,0:T(8,128)(2,1)S(1)} copy-done((bf16[128,256]{1,0:T(8,128)(2,1)S(1)}, bf16[128,256]{1,0:T(8,128)(2,1)}, u32[]{:S(2)}) %copy-start.2) | copy-done | bytes 65560
  26.9 0.0 copy-start.3
  26.9 0.9 %copy-done.3 = bf16[16,64,64]{2,1,0:T(8,128)(2,1)S(1)} copy-done((bf16[16,64,64]{2,1,0:T(8,128)(2,1)S(1)}, bf16[16,64,64]{2,1,0:T(8,128)(2,1)}, u32[]{:S(2)}) %copy-start.3) | copy-done | bytes 131096
  27.8 0.0 copy-start.5
  27.8 0.7 %copy-done.5 = s32[96,9]{0,1:T(8,128)S(1)} copy-done((s32[96,9]{0,1:T(8,128)S(1)}, s32[96,9]{0,1:T(8,128)}, u32[]{:S(2)}) %copy-start.5) | copy-done | bytes 3480
  28.5 0.0 copy-start.6
  28.5 0.7 %copy-done.6 = s32[96,9]{0,1:T(8,128)S(1)} copy-done((s32[96,9]{0,1:T(8,128)S(1)}, s32[96,9]{0,1:T(8,128)}, u32[]{:S(2)}) %copy-start.6) | copy-done | bytes 3480
  29.2 0.0 copy-start.7
  29.2 0.7 %copy-done.7 = f32[96,9]{0,1:T(8,128)S(1)} copy-done((f32[96,9]{0,1:T(8,128)S(1)}, f32[96,9]{0,1:T(8,128)}, u32[]{:S(2)}) %copy-start.7) | copy-done | bytes 3480
  29.9 10.9 %mass_product.1 = (bf16[6144,256]{1,0:T(8,128)(2,1)}, f32[32,4,128]{2,1,0:T(4,128)S(1)}) custom-call(s32[1]{0:T(128)S(6)} %copy.11.owned, s32[9,96]{1,0:T(8,128)S(1)} %bitcast.7, s32[9,96]{1,0:T(8,128)S(1)} %bitcast.8, f32[9,96]{1,0:T(8,128)S(1)} %bitcast.9, bf16[96,64,128]{2,1,0:T(8,128)(2,1)S(1)} %bitcast.5, bf16[32,64,128]{2,1,0:T(8,128)(2,1)S(1)} %bitcast.6, ...), custom_call_target="tpu_custom_call" | custom-call | tf_op jit(solution)/shard_map/mass_product/pallas_call | solution.py:166
  40.8 27.1 %gram_total.1 = f32[128,256]{1,0:T(8,128)S(1)} custom-call(f32[32,4,128]{2,1,0:T(4,128)S(1)} %get-tuple-element.5.gram, bf16[128,256]{1,0:T(8,128)(2,1)S(1)} %copy-done.2), custom_call_target="tpu_custom_call" | custom-call | tf_op jit(solution)/shard_map/gram_total/pallas_call | solution.py:297
  68.0 0.7 copy.12
Async XLA Ops:
  1.3 1.4 %copy-start = (bf16[6144,128]{1,0:T(8,128)(2,1)S(1)}, bf16[6144,128]{1,0:T(8,128)(2,1)}, u32[]{:S(2)}) copy-start(bf16[6144,128]{1,0:T(8,128)(2,1)} %snap_hbm.1) | copy-start | bytes 4718596
  2.7 0.7 %copy-start.4 = (s32[1,4,512]{2,1,0:T(4,128)S(1)}, s32[1,4,512]{2,1,0:T(4,128)}, u32[]{:S(2)}) copy-start(s32[1,4,512]{2,1,0:T(4,128)} %lists.1) | copy-start | bytes 24580
  3.4 22.6 %copy-start.1 = (bf16[6144,128]{1,0:T(8,128)(2,1)S(1)}, bf16[6144,128]{1,0:T(8,128)(2,1)}, u32[]{:S(2)}) copy-start(bf16[6144,128]{1,0:T(8,128)(2,1)} %snap_hbm.1) | copy-start | bytes 4718596
  26.0 0.8 %copy-start.2 = (bf16[128,256]{1,0:T(8,128)(2,1)S(1)}, bf16[128,256]{1,0:T(8,128)(2,1)}, u32[]{:S(2)}) copy-start(bf16[128,256]{1,0:T(8,128)(2,1)} %test.3) | copy-start | bytes 196612
  26.9 0.9 %copy-start.3 = (bf16[16,64,64]{2,1,0:T(8,128)(2,1)S(1)}, bf16[16,64,64]{2,1,0:T(8,128)(2,1)}, u32[]{:S(2)}) copy-start(bf16[16,64,64]{2,1,0:T(8,128)(2,1)} %table.1) | copy-start | bytes 393220
  27.8 0.7 %copy-start.5 = (s32[96,9]{0,1:T(8,128)S(1)}, s32[96,9]{0,1:T(8,128)}, u32[]{:S(2)}) copy-start(s32[96,9]{0,1:T(8,128)} %param.11) | copy-start | bytes 10372
  28.5 0.7 %copy-start.6 = (s32[96,9]{0,1:T(8,128)S(1)}, s32[96,9]{0,1:T(8,128)}, u32[]{:S(2)}) copy-start(s32[96,9]{0,1:T(8,128)} %param.12) | copy-start | bytes 10372
  29.2 0.7 %copy-start.7 = (f32[96,9]{0,1:T(8,128)S(1)}, f32[96,9]{0,1:T(8,128)}, u32[]{:S(2)}) copy-start(f32[96,9]{0,1:T(8,128)} %param.13) | copy-start | bytes 10372

commit v2 on v1

--- a/solution.py
+++ b/solution.py
@@ -9,7 +9,8 @@
 
 MESH = pl.DeviceIdType.MESH
 NEAR = 2
-MIB = 1 << 20
+GRANT = 64 << 20
+CHUNKS = 4
 
 
 def rows_kernel(
@@ -22,20 +23,26 @@
     right, left = lax.rem(g + 1, group_n), lax.rem(g + group_n - 1, group_n)
     plan = ((1, (above, g)), (0, (below, g)), (3, (b, right)), (2, (b, left)))
 
-    load = pltpu.make_async_copy(snap_hbm, snap, load_sem)
-    load.start()
+    chunk = row_count // CHUNKS
+    loads = [
+        pltpu.make_async_copy(snap_hbm.at[rows], snap.at[rows], load_sem.at[n])
+        for n, rows in enumerate(pl.ds(i * chunk, chunk) for i in range(CHUNKS))
+    ]
+    for load in loads:
+        load.start()
     barrier = pltpu.get_barrier_semaphore()
     for _, peer in plan:
         pl.semaphore_signal(barrier, inc=1, device_id=peer, device_id_type=MESH)
-    load.wait()
-    step = 256
+    step = 128
 
     def widen(i, carry):
         rows = pl.ds(pl.multiple_of(i * step, step), step)
         wide[rows, :] = snap[rows, :].astype(jnp.float32)
         return carry
 
-    lax.fori_loop(0, row_count // step, widen, 0)
+    for n, load in enumerate(loads):
+        load.wait()
+        lax.fori_loop(n * chunk // step, (n + 1) * chunk // step, widen, 0)
     pl.semaphore_wait(barrier, len(plan))
 
     copies = []
@@ -76,12 +83,12 @@
             pltpu.VMEM((rows, snaps), jnp.float32),
             pltpu.VMEM((faces, snaps), jnp.float32),
             pltpu.VMEM((4, faces, snaps), jnp.bfloat16),
-            pltpu.SemaphoreType.DMA,
+            pltpu.SemaphoreType.DMA((CHUNKS,)),
             pltpu.SemaphoreType.DMA((4,)),
             pltpu.SemaphoreType.DMA((4,)),
         ],
         compiler_params=pltpu.CompilerParams(
-            collective_id=0, has_side_effects=True, vmem_limit_bytes=24 * MIB
+            collective_id=0, has_side_effects=True, vmem_limit_bytes=GRANT
         ),
         name="ghost_rows",
     )(iface_lists, snapshots)
@@ -187,7 +194,7 @@
             pltpu.VMEM((per_step * block, snaps), jnp.bfloat16),
             pltpu.VMEM((snaps, snaps), jnp.float32),
         ],
-        compiler_params=pltpu.CompilerParams(vmem_limit_bytes=32 * MIB),
+        compiler_params=pltpu.CompilerParams(vmem_limit_bytes=GRANT),
         name="mass_product",
     )(
         owned, columns.T, types.T, scales.T,
@@ -197,84 +204,57 @@
     )
 
 
+def wrapped(index, count):
+    return jnp.where(index >= count, index - count, index)
+
+
 def total_kernel(
-    bulk_n, group_n, divisor, gram, test, sketch,
-    near, far, whole, full, send_a, recv_a, send_b, recv_b, send_c, recv_c,
+    bulk_n, group_n, divisor, gram, test, sketch, near, far, whole, full, send_sem, recv_sem
 ):
     parts, height, snaps = gram.shape
     depth = bulk_n // NEAR
     b, g = lax.axis_index("bulk"), lax.axis_index("group")
-    z, q = b // NEAR, lax.rem(b, NEAR) * group_n + g
+    z, y = b // NEAR, lax.rem(b, NEAR)
+    q = y * group_n + g
 
     def in_plane(d):
-        other = lax.rem(q + d, parts)
-        return other, (z * NEAR + other // group_n, lax.rem(other, group_n))
+        other = wrapped(q + d, parts)
+        up = sum((other >= n * group_n).astype(jnp.int32) for n in range(1, NEAR))
+        return other, (z * NEAR + up, other - up * group_n)
 
     def along_z(d):
-        other = lax.rem(z + d, depth)
-        return other, (other * NEAR + lax.rem(b, NEAR), g)
+        other = wrapped(z + d, depth)
+        return other, (other * NEAR + y, g)
 
     barrier = pltpu.get_barrier_semaphore()
-
-    def greet(where):
-        def body(d, carry):
-            _, peer = where(d)
-            pl.semaphore_signal(barrier, inc=1, device_id=peer, device_id_type=MESH)
-            return carry
-        return body
-
-    lax.fori_loop(1, parts, greet(in_plane), 0)
-    lax.fori_loop(1, depth, greet(along_z), 0)
+    for where, count in ((in_plane, parts), (along_z, depth)):
+        for d in range(1, count):
+            pl.semaphore_signal(barrier, inc=1, device_id=where(d)[1], device_id_type=MESH)
     near[pl.ds(q, 1)] = gram[pl.ds(q, 1)]
     pl.semaphore_wait(barrier, parts + depth - 2)
 
-    def scatter(d):
-        other, peer = in_plane(d)
+    def copy(phase, source, target, peer):
         return pltpu.make_async_remote_copy(
-            src_ref=gram.at[other], dst_ref=near.at[q], send_sem=send_a.at[d], recv_sem=recv_a.at[d],
+            src_ref=source, dst_ref=target, send_sem=send_sem.at[phase], recv_sem=recv_sem.at[phase],
             device_id=peer, device_id_type=MESH,
         )
 
-    def spread(d):
-        _, peer = along_z(d)
-        return pltpu.make_async_remote_copy(
-            src_ref=far.at[z], dst_ref=far.at[z], send_sem=send_b.at[d], recv_sem=recv_b.at[d],
-            device_id=peer, device_id_type=MESH,
-        )
-
-    def gather(d):
-        _, peer = in_plane(d)
-        return pltpu.make_async_remote_copy(
-            src_ref=whole.at[q], dst_ref=whole.at[q], send_sem=send_c.at[d], recv_sem=recv_c.at[d],
-            device_id=peer, device_id_type=MESH,
-        )
-
-    def start(make):
-        def body(d, carry):
-            make(d).start()
-            return carry
-        return body
-
-    def arrive(make):
-        def body(d, carry):
-            make(d).wait_recv()
-            return carry
-        return body
-
-    def leave(make):
-        def body(d, carry):
-            make(d).wait_send()
-            return carry
-        return body
-
-    lax.fori_loop(1, parts, start(scatter), 0)
-    lax.fori_loop(1, parts, arrive(scatter), 0)
+    def all_of(phase, buffer):
+        some = buffer.at[pl.ds(0, buffer.shape[0] - 1)]
+        return copy(phase, some, some, (b, g))
+
+    for d in range(1, parts):
+        other, peer = in_plane(d)
+        copy(0, gram.at[other], near.at[q], peer).start()
+    all_of(0, near).wait_recv()
     far[pl.ds(z, 1)] = jnp.sum(near[...], axis=0, keepdims=True)
-    lax.fori_loop(1, depth, start(spread), 0)
-    lax.fori_loop(1, depth, arrive(spread), 0)
+    for d in range(1, depth):
+        copy(1, far.at[z], far.at[z], along_z(d)[1]).start()
+    all_of(1, far).wait_recv()
     whole[pl.ds(q, 1)] = jnp.sum(far[...], axis=0, keepdims=True)
-    lax.fori_loop(1, parts, start(gather), 0)
-    lax.fori_loop(1, parts, arrive(gather), 0)
+    for d in range(1, parts):
+        copy(2, whole.at[q], whole.at[q], in_plane(d)[1]).start()
+    all_of(2, whole).wait_recv()
     for p in range(parts):
         full[p * height : (p + 1) * height, :] = whole[p]
     sketch[...] = (
@@ -284,9 +264,9 @@
         )
         / divisor
     )
-    lax.fori_loop(1, parts, leave(scatter), 0)
-    lax.fori_loop(1, depth, leave(spread), 0)
-    lax.fori_loop(1, parts, leave(gather), 0)
+    all_of(0, near).wait_send()
+    all_of(1, far).wait_send()
+    all_of(2, whole).wait_send()
 
 
 def summed_sketch(gram, test, divisor, bulk_n, group_n):
@@ -304,15 +284,11 @@
             pltpu.VMEM((depth, height, snaps), jnp.float32),
             pltpu.VMEM((parts, height, snaps), jnp.float32),
             pltpu.VMEM((snaps, snaps), jnp.float32),
-            pltpu.SemaphoreType.DMA((parts,)),
-            pltpu.SemaphoreType.DMA((parts,)),
-            pltpu.SemaphoreType.DMA((depth,)),
-            pltpu.SemaphoreType.DMA((depth,)),
-            pltpu.SemaphoreType.DMA((parts,)),
-            pltpu.SemaphoreType.DMA((parts,)),
+            pltpu.SemaphoreType.DMA((3,)),
+            pltpu.SemaphoreType.DMA((3,)),
         ],
         compiler_params=pltpu.CompilerParams(
-            collective_id=1, has_side_effects=True, vmem_limit_bytes=16 * MIB
+            collective_id=1, has_side_effects=True, vmem_limit_bytes=GRANT
         ),
         name="gram_total",
     )(gram, test)

time: 69 us -> 63.4 us (0.919)
  local copies, waits for them, and re-layouts: 6.63 us -> 1.57 us
    unnamed x17 -> x1, local copies, waits for them, and re-layouts: 6.63 us -> 1.57 us
    pallas_call x1, Pallas kernels: 27.1 us -> 25.9 us  [summed_sketch(): pl.pallas_call(functools.partial(total_kernel, bulk_n, group_n, divisor),...]
    pallas_call x1, Pallas kernels: 10.9 us -> 11.6 us  [mass_product(): pl.pallas_call(functools.partial(mass_kernel, edges, entries), grid=(own...]
where the time goes in v2:
time: 63.4 us; the launch traced here: 63 us
  Pallas kernels  60.2 us (95%)
  local copies, waits for them, and re-layouts  1.57 us (2%)
  between operations  1.29 us (2%)
    pallas_call x1, Pallas kernels, summed_sketch(): pl.pallas_call(functools.partial(total_kernel, bulk_n, group_n, divisor),...  25.9 us
    pallas_call x1, Pallas kernels, exchanged(): pl.pallas_call(functools.partial(rows_kernel, bulk_n, group_n), out_shape...  22.6 us
    pallas_call x1, Pallas kernels, mass_product(): pl.pallas_call(functools.partial(mass_kernel, edges, entries), grid=(own...  11.6 us
    unnamed x1, local copies, waits for them, and re-layouts  1.57 us

profile of v2, /device:TPU:1, one launch (start us, length us, event | category | flops | bytes accessed | tf_op | source)
XLA Modules:
  0.0 63.0 jit_solution(17195456712120275232)
XLA Ops:
  1.3 22.6 %ghost_rows.1 = bf16[4,512,128]{2,1,0:T(8,128)(2,1)} custom-call(s32[1,4,512]{2,1,0:T(4,128)} %lists.1, bf16[6144,128]{1,0:T(8,128)(2,1)} %snap_hbm.1), custom_call_target="tpu_custom_call" | custom-call | tf_op jit(solution)/shard_map/ghost_rows/pallas_call | solution.py:76
  23.9 11.6 %mass_product.1 = (bf16[6144,256]{1,0:T(8,128)(2,1)}, f32[32,4,128]{2,1,0:T(4,128)}) custom-call(s32[1]{0:T(128)S(6)} %copy.11.owned, s32[9,96]{1,0:T(8,128)} %bitcast.7, s32[9,96]{1,0:T(8,128)} %bitcast.8, f32[9,96]{1,0:T(8,128)} %bitcast.9, bf16[96,64,128]{2,1,0:T(8,128)(2,1)} %bitcast.5, bf16[32,64,128]{2,1,0:T(8,128)(2,1)} %bitcast.6, ...), custom_call_target="tpu_custom_call" | custom-call | tf_op jit(solution)/shard_map/mass_product/pallas_call | solution.py:173
  35.6 25.9 %gram_total.1 = f32[128,256]{1,0:T(8,128)} custom-call(f32[32,4,128]{2,1,0:T(4,128)} %get-tuple-element.5.gram, bf16[128,256]{1,0:T(8,128)(2,1)} %test.3), custom_call_target="tpu_custom_call" | custom-call | tf_op jit(solution)/shard_map/gram_total/pallas_call | solution.py:277
  61.5 1.6 %copy.12 = f32[128,256]{1,0:T(8,128)} copy(f32[128,256]{1,0:T(8,128)} %gram_total.1) | data formatting | bytes 262144

commit v3 on v0

v3 whole, which is shorter than its diff:
```python
import functools

import jax
import jax.numpy as jnp
from jax import lax
from jax.experimental import pallas as pl
from jax.experimental.pallas import tpu as pltpu
from jax.sharding import PartitionSpec as P

MESH = pl.DeviceIdType.MESH
NEAR = 2
GRANT = 64 << 20
PIECES = 12
CHUNKS = 4
STEP = 8
WIDE = 4


def wrapped(index, count):
    return jnp.where(index >= count, index - count, index)


def partition_kernel(
    bulk_n, group_n, owned, lists_hbm, columns_hbm, types_hbm, scales_hbm, snap_hbm, table_hbm, test_hbm,
    projected_hbm, summed, lists, columns, types, scales, table, test,
    cols, wide, picked, packed, pairs, scaled, weighted, projected, total, gram, near, far,
    load_sem, late_sem, ghost_send, ghost_recv, sum_send, sum_recv, store_sem,
):
    own, block, snaps = snap_hbm.shape
    faces = picked.shape[0]
    face_blocks = faces // block
    entries = columns.shape[0]
    parts, height, _ = gram.shape
    depth = bulk_n // NEAR
    count = owned[0]
    b, g = lax.axis_index("bulk"), lax.axis_index("group")
    z, y = b // NEAR, lax.rem(b, NEAR)
    q = y * group_n + g
    line = lax.broadcasted_iota(jnp.int32, (block, snaps), 0)

    def in_plane(d):
        other = wrapped(q + d, parts)
        up = (other >= group_n).astype(jnp.int32)
        return other, (z * NEAR + up, other - up * group_n)

    def along_z(d):
        return (wrapped(z + d, depth) * NEAR + y, g)

    above, below = lax.rem(b + 1, bulk_n), lax.rem(b + bulk_n - 1, bulk_n)
    right, left = lax.rem(g + 1, group_n), lax.rem(g + group_n - 1, group_n)
    plan = ((1, (above, g)), (0, (below, g)), (3, (b, right)), (2, (b, left)))

    chunk = own // CHUNKS
    loads = [
        pltpu.make_async_copy(
            snap_hbm.at[pl.ds(n * chunk, chunk)], cols.at[pl.ds(n * chunk, chunk)], load_sem.at[n]
        )
        for n in range(CHUNKS)
    ]
    early = pltpu.make_async_copy(lists_hbm, lists, load_sem.at[CHUNKS])
    late = [
        pltpu.make_async_copy(source, target, late_sem.at[n])
        for n, (source, target) in enumerate(
            (
                (columns_hbm, columns), (types_hbm, types), (scales_hbm, scales),
                (table_hbm, table), (test_hbm, test),
            )
        )
    ]
    for load in [early] + loads + late:
        load.start()

    barrier = pltpu.get_barrier_semaphore()
    slanted = jnp.where(y == 0, below, above)
    peers = [(slanted, g)] + [in_plane(d)[1] for d in range(1, parts)]
    peers += [along_z(d) for d in range(1, depth)]
    for peer in peers:
        pl.semaphore_signal(barrier, inc=1, device_id=peer, device_id_type=MESH)

    def widen(i, carry):
        for u in range(WIDE):
            r = i * WIDE + u
            wide[pl.ds(pl.multiple_of(r * block, block), block), :] = cols[r].astype(jnp.float32)
        return carry

    for n, load in enumerate(loads):
        load.wait()
        lax.fori_loop(n * chunk // WIDE, (n + 1) * chunk // WIDE, widen, 0)

    early.wait()
    ghosts = []
    for slot, (which, peer) in enumerate(plan):

        def pick(i, carry):
            for u in range(16):
                r = i * 16 + u
                picked[pl.ds(r, 1), :] = wide[pl.ds(lists[0, which, r], 1), :]
            return carry

        lax.fori_loop(0, faces // 16, pick, 0)
        packed[slot] = picked[...].astype(jnp.bfloat16).reshape(face_blocks, block, snaps)
        copy = pltpu.make_async_remote_copy(
            src_ref=packed.at[slot],
            dst_ref=cols.at[pl.ds(own + slot * face_blocks, face_blocks)],
            send_sem=ghost_send.at[slot],
            recv_sem=ghost_recv.at[slot],
            device_id=peer,
            device_id_type=MESH,
        )
        if slot == 0:
            pl.semaphore_wait(barrier, len(peers))
        copy.start()
        ghosts.append(copy)

    for load in late:
        load.wait()
    lane = lax.broadcasted_iota(jnp.int32, (1, 2 * block), 1) < block
    for t in range(table.shape[0]):
        both = table[t].astype(jnp.float32)
        pairs[t] = jnp.concatenate([both, both], axis=1)

    def scale_row(i, carry):
        for u in range(WIDE):
            r = i * WIDE + u
            kept = line + r * block < count
            cols[r] = jnp.where(kept, cols[r].astype(jnp.float32), 0.0).astype(jnp.bfloat16)
            for k in range(0, entries - 1, 2):
                one, two = pairs[types[k, r]], pairs[types[k + 1, r]]
                factor = jnp.where(lane, scales[k, r], scales[k + 1, r])
                tile = (jnp.where(lane, one, two) * factor).astype(jnp.bfloat16)
                scaled[r, :, k * block : (k + 2) * block] = tile
            if entries % 2:
                last = pairs[types[entries - 1, r]][:, :block] * scales[entries - 1, r]
                scaled[r, :, (entries - 1) * block :] = last.astype(jnp.bfloat16)
        return carry

    lax.fori_loop(0, own // WIDE, scale_row, 0)
    total[...] = jnp.zeros_like(total)
    weighted[pl.ds(0, STEP)] = jnp.zeros((STEP, block, snaps), jnp.bfloat16)
    for copy in ghosts:
        copy.wait()
    for slot, edge in ((0, 0), (1, bulk_n - 1)):

        @pl.when(b == edge)
        def _():
            first = own + slot * face_blocks
            cols[first : first + face_blocks] = jnp.zeros((face_blocks, block, snaps), jnp.bfloat16)

    def gram_step(i):
        rows = pl.ds(i * STEP, STEP)
        total[...] += lax.dot_general(
            cols[rows].reshape(STEP * block, snaps), weighted[rows].reshape(STEP * block, snaps),
            (((0,), (0,)), ((), ())), preferred_element_type=jnp.float32,
        )

    def mass_step(i, carry):
        gram_step(jnp.maximum(i - 1, 0))
        for u in range(STEP):
            r = i * STEP + u
            stacked = jnp.concatenate([cols[columns[k, r]] for k in range(entries)], axis=0)
            value = jnp.dot(scaled[r], stacked, preferred_element_type=jnp.float32)
            keep = line + r * block < count
            weighted[r] = jnp.where(keep, value, 0.0).astype(jnp.bfloat16)
        return carry

    lax.fori_loop(0, own // STEP, mass_step, 0)
    gram_step(own // STEP - 1)

    def project(phase):
        def one(i, carry):
            here = weighted[pl.ds(i * STEP, STEP)].reshape(STEP * block, snaps)
            rows = pl.ds(pl.multiple_of(i * (STEP * block), STEP * block), STEP * block)
            product = jnp.dot(here, test[...], preferred_element_type=jnp.float32)
            projected[rows, :] = product.astype(jnp.bfloat16)
            return carry

        steps = own // STEP
        first, last = phase * steps // 3, (phase + 1) * steps // 3
        lax.fori_loop(first, last, one, 0)
        rows = pl.ds(first * STEP * block, (last - first) * STEP * block)
        store = pltpu.make_async_copy(projected.at[rows], projected_hbm.at[rows], store_sem.at[phase])
        store.start()
        return store

    for p in range(parts):
        gram[p] = total[p * height : (p + 1) * height, :]
    near[pl.ds(q, 1)] = gram[pl.ds(q, 1)]

    def copy(phase, source, target, peer):
        return pltpu.make_async_remote_copy(
            src_ref=source, dst_ref=target, send_sem=sum_send.at[phase], recv_sem=sum_recv.at[phase],
            device_id=peer, device_id_type=MESH,
        )

    def all_of(phase, buffer):
        some = buffer.at[pl.ds(0, buffer.shape[0] - 1)]
        return copy(phase, some, some, (b, g))

    for d in range(1, parts):
        other, peer = in_plane(d)
        copy(0, gram.at[other], near.at[q], peer).start()
    stores = [project(0)]
    all_of(0, near).wait_recv()
    far[pl.ds(z, 1)] = jnp.sum(near[...], axis=0, keepdims=True)
    for d in sorted(range(1, depth), key=lambda d: -min(d, depth - d)):
        copy(1, far.at[z], far.at[z], along_z(d)).start()
    stores.append(project(1))
    all_of(1, far).wait_recv()
    summed[pl.ds(q, 1)] = jnp.sum(far[...], axis=0, keepdims=True)
    for d in range(1, parts):
        copy(2, summed.at[q], summed.at[q], in_plane(d)[1]).start()
    stores.append(project(2))
    all_of(2, summed).wait_recv()
    all_of(0, near).wait_send()
    all_of(1, far).wait_send()
    all_of(2, summed).wait_send()
    for store in stores:
        store.wait()


def partition_terms(
    snapshots, owned, lists, columns, types, scales, table, test, bulk_n, group_n
):
    rows, snaps = snapshots.shape
    kinds, block, _ = table.shape
    own, entries = columns.shape
    faces = lists.shape[2]
    outer = 4 * faces // block
    parts, depth = NEAR * group_n, bulk_n // NEAR
    height = snaps // parts
    scalar = pl.BlockSpec(memory_space=pltpu.SMEM)
    vmem = pl.BlockSpec(memory_space=pltpu.VMEM)
    return pl.pallas_call(
        functools.partial(partition_kernel, bulk_n, group_n),
        out_shape=(
            jax.ShapeDtypeStruct((rows, test.shape[1]), jnp.bfloat16),
            jax.ShapeDtypeStruct((parts, height, snaps), jnp.float32),
        ),
        in_specs=[scalar] + [pl.BlockSpec(memory_space=pl.ANY)] * 7,
        out_specs=(pl.BlockSpec(memory_space=pl.ANY), vmem),
        scratch_shapes=[
            pltpu.SMEM(lists.shape, jnp.int32),
            pltpu.SMEM((entries, own), jnp.int32),
            pltpu.SMEM((entries, own), jnp.int32),
            pltpu.SMEM((entries, own), jnp.float32),
            pltpu.VMEM(table.shape, table.dtype),
            pltpu.VMEM(test.shape, test.dtype),
            pltpu.VMEM((own + outer, block, snaps), jnp.bfloat16),
            pltpu.VMEM((rows, snaps), jnp.float32),
            pltpu.VMEM((faces, snaps), jnp.float32),
            pltpu.VMEM((4, faces // block, block, snaps), jnp.bfloat16),
            pltpu.VMEM((kinds, block, 2 * block), jnp.float32),
            pltpu.VMEM((own, block, entries * block), jnp.bfloat16),
            pltpu.VMEM((own, block, snaps), jnp.bfloat16),
            pltpu.VMEM((rows, test.shape[1]), jnp.bfloat16),
            pltpu.VMEM((snaps, snaps), jnp.float32),
            pltpu.VMEM((parts, height, snaps), jnp.float32),
            pltpu.VMEM((parts, height, snaps), jnp.float32),
            pltpu.VMEM((depth, height, snaps), jnp.float32),
            pltpu.SemaphoreType.DMA((CHUNKS + 1,)),
            pltpu.SemaphoreType.DMA((5,)),
            pltpu.SemaphoreType.DMA((4,)),
            pltpu.SemaphoreType.DMA((4,)),
            pltpu.SemaphoreType.DMA((3,)),
            pltpu.SemaphoreType.DMA((3,)),
            pltpu.SemaphoreType.DMA((3,)),
        ],
        compiler_params=pltpu.CompilerParams(
            collective_id=0, has_side_effects=True, vmem_limit_bytes=GRANT
        ),
        name="partition_terms",
    )(owned, lists, columns.T, types.T, scales.T, snapshots.reshape(own, block, snaps), table, test)


def outputs_kernel(divisor, made, summed_hbm, test_hbm, projected, sketch_hbm, held, summed, test, full, sketch, sems, out_sems):
    small = [
        pltpu.make_async_copy(summed_hbm, summed, sems.at[PIECES]),
        pltpu.make_async_copy(test_hbm, test, sems.at[PIECES + 1]),
    ]
    size = made.shape[0] // PIECES
    pieces = [pl.ds(n * size, size) for n in range(PIECES)]
    loads = [pltpu.make_async_copy(made.at[p], held.at[p], sems.at[n]) for n, p in enumerate(pieces)]
    stores = [pltpu.make_async_copy(held.at[p], projected.at[p], out_sems.at[n]) for n, p in enumerate(pieces)]
    for copy in small + loads:
        copy.start()
    for load, store in zip(loads, stores):
        load.wait()
        store.start()
    for copy in small:
        copy.wait()
    parts, height, _ = summed.shape
    for p in range(parts):
        full[p * height : (p + 1) * height, :] = summed[p]
    product = jnp.dot(
        full[...], test[...].astype(jnp.float32),
        precision=lax.Precision.HIGHEST, preferred_element_type=jnp.float32,
    )
    sketch[...] = product / divisor
    last = pltpu.make_async_copy(sketch, sketch_hbm, sems.at[PIECES + 2])
    last.start()
    for copy in stores + [last]:
        copy.wait()


def final_outputs(made, summed, test):
    rows, width = made.shape
    snaps = test.shape[0]
    anywhere = pl.BlockSpec(memory_space=pl.ANY)
    return pl.pallas_call(
        functools.partial(outputs_kernel, rows),
        out_shape=(
            jax.ShapeDtypeStruct((rows, width), jnp.bfloat16),
            jax.ShapeDtypeStruct((snaps, width), jnp.float32),
        ),
        in_specs=[anywhere] * 3,
        out_specs=(anywhere, anywhere),
        scratch_shapes=[
            pltpu.VMEM(made.shape, made.dtype),
            pltpu.VMEM(summed.shape, jnp.float32),
            pltpu.VMEM(test.shape, jnp.bfloat16),
            pltpu.VMEM((snaps, snaps), jnp.float32),
            pltpu.VMEM((snaps, width), jnp.float32),
            pltpu.SemaphoreType.DMA((PIECES + 3,)),
            pltpu.SemaphoreType.DMA((PIECES,)),
        ],
        compiler_params=pltpu.CompilerParams(vmem_limit_bytes=GRANT),
        name="final_outputs",
    )(made, summed, test)


def on_device(
    bulk_n, group_n,
    snapshots, owned_rows, iface_lists, block_columns, block_types, block_scales, mass_table, sketch_matrix,
):
    made, summed = partition_terms(
        snapshots, owned_rows, iface_lists, block_columns, block_types, block_scales, mass_table,
        sketch_matrix, bulk_n, group_n,
    )
    return final_outputs(made, summed, sketch_matrix)


def solution(mesh):
    return jax.shard_map(
        functools.partial(on_device, mesh.shape["bulk"], mesh.shape["group"]),
        mesh=mesh,
        in_specs=(
            P(("bulk", "group"), None),
            P(("bulk", "group")),
            P(("bulk", "group"), None, None),
            P(("bulk", "group"), None),
            P(("bulk", "group"), None),
            P(("bulk", "group"), None),
            P(),
            P(),
        ),
        out_specs=(P(("bulk", "group"), None), P()),
        check_vma=False,
    )
```

time: 590 us -> 53 us (0.09)
  waiting for transfers between devices: 455 us -> 0 us
  Pallas kernels: 0 us -> 51.5 us
  local copies, waits for them, and re-layouts: 46.6 us -> 0 us
  matrix products: 39.3 us -> 0 us
  other arithmetic: 18.2 us -> 0 us
  between operations: 14.8 us -> 1.28 us
  starting transfers between devices: 13.5 us -> 0 us
    psum x1 -> x0, waiting for transfers between devices: 455 us -> none  [on_device(): sketch = lax.psum(local_sketch, ('bulk', 'group')) / row_count]
    pallas_call x0 -> x2, Pallas kernels: none -> 51.5 us  [the longest x1 48.5 us: partition_terms(): pl.pallas_call(functools.partial(partition_kernel, bulk_n, group_n), out_...]
    dot_general x12 -> x0, matrix products: 39.3 us -> none  [the longest x9 35.2 us: add_entry(): jnp.einsum('bij,bjs->bis', ref_tiles, gathered, preferred_element_type=jn...]
    gather x19 -> x0, local copies, waits for them, and re-layouts: 35.8 us -> none  [the longest x9 22 us: add_entry(): gathered = node_blocks[column_ids]]
    ppermute x4 -> x0, starting transfers between devices: 13.4 us -> none  [the longest x2 7.34 us: extended(): lax.ppermute(head, axis, [((i + 1) % count, i) for i in range(ends)])]
    select_n x10 -> x0, other arithmetic: 6.4 us -> none  [the longest x9 6.39 us: add_entry(): ref_tiles = mass_table[type_ids]]
    mul x9 -> x0, local copies, waits for them, and re-layouts: 6.22 us -> none  [add_entry(): return (accumulated + jacobians[:, None, None] * term_value, None)]
  transfers between devices with their start and end apart: 5 -> 0, of which waited for: 2 -> 0; matrix products, arithmetic and copies ran while one was open for 1% -> 0% of each run, Pallas kernels for 0% -> 0%
where the time goes in v3:
time: 53 us; the launch traced here: 52.8 us
  Pallas kernels  51.5 us (97%)
  between operations  1.28 us (2%)
    pallas_call x1, Pallas kernels, partition_terms(): pl.pallas_call(functools.partial(partition_kernel, bulk_n, group_n), out_...  48.5 us
    pallas_call x1, Pallas kernels, final_outputs(): pl.pallas_call(functools.partial(outputs_kernel, rows), out_shape=(jax.Sh...  3.04 us

profile of v3, /device:TPU:1, one launch (start us, length us, event | category | flops | bytes accessed | tf_op | source)
XLA Modules:
  0.0 52.8 jit_solution(391100612675653425)
XLA Ops:
  1.3 48.5 %partition_terms.1 = (bf16[6144,256]{1,0:T(8,128)(2,1)}, f32[32,4,128]{2,1,0:T(4,128)}) custom-call(s32[1]{0:T(128)S(6)} %copy.10.owned, s32[1,4,512]{2,1,0:T(4,128)} %lists_hbm.1, s32[9,96]{1,0:T(8,128)} %bitcast.5, s32[9,96]{1,0:T(8,128)} %bitcast.6, f32[9,96]{1,0:T(8,128)} %bitcast.7, bf16[96,64,128]{2,1,0:T(8,128)(2,1)} %bitcast.4, ...), custom_call_target="tpu_custom_call" | custom-call | tf_op jit(solution)/shard_map/partition_terms/pallas_call | solution.py:233
  49.7 3.0 %final_outputs.1 = (bf16[6144,256]{1,0:T(8,128)(2,1)}, f32[128,256]{1,0:T(8,128)}) custom-call(bf16[6144,256]{1,0:T(8,128)(2,1)} %get-tuple-element.4.made, f32[32,4,128]{2,1,0:T(4,128)} %get-tuple-element.5.summed_hbm, bf16[128,256]{1,0:T(8,128)(2,1)} %test_hbm.3), custom_call_target="tpu_custom_call" | custom-call | tf_op jit(solution)/shard_map/final_outputs/pallas_call | solution.py:309

commit v4 on v3

--- a/solution.py
+++ b/solution.py
@@ -10,9 +10,11 @@
 MESH = pl.DeviceIdType.MESH
 NEAR = 2
 GRANT = 64 << 20
+ROOM = 16 << 20
 PIECES = 12
 CHUNKS = 4
-STEP = 8
+HALVES = 2
+STEP = 16
 WIDE = 4
 
 
@@ -22,13 +24,12 @@
 
 def partition_kernel(
     bulk_n, group_n, owned, lists_hbm, columns_hbm, types_hbm, scales_hbm, snap_hbm, table_hbm, test_hbm,
-    projected_hbm, summed, lists, columns, types, scales, table, test,
-    cols, wide, picked, packed, pairs, scaled, weighted, projected, total, gram, near, far,
-    load_sem, late_sem, ghost_send, ghost_recv, sum_send, sum_recv, store_sem,
+    projected, summed, lists, columns, types, scales, table, test,
+    cols, wide, picked, packed, pairs, scaled, weighted, total, gram, near, far,
+    load_sem, late_sem, ghost_send, ghost_recv, sum_send, sum_recv,
 ):
     own, block, snaps = snap_hbm.shape
-    faces = picked.shape[0]
-    face_blocks = faces // block
+    face_blocks = packed.shape[1]
     entries = columns.shape[0]
     parts, height, _ = gram.shape
     depth = bulk_n // NEAR
@@ -89,28 +90,33 @@
 
     early.wait()
     ghosts = []
+    half = face_blocks // HALVES
     for slot, (which, peer) in enumerate(plan):
-
-        def pick(i, carry):
-            for u in range(16):
-                r = i * 16 + u
-                picked[pl.ds(r, 1), :] = wide[pl.ds(lists[0, which, r], 1), :]
-            return carry
-
-        lax.fori_loop(0, faces // 16, pick, 0)
-        packed[slot] = picked[...].astype(jnp.bfloat16).reshape(face_blocks, block, snaps)
-        copy = pltpu.make_async_remote_copy(
-            src_ref=packed.at[slot],
-            dst_ref=cols.at[pl.ds(own + slot * face_blocks, face_blocks)],
-            send_sem=ghost_send.at[slot],
-            recv_sem=ghost_recv.at[slot],
-            device_id=peer,
-            device_id_type=MESH,
-        )
-        if slot == 0:
-            pl.semaphore_wait(barrier, len(peers))
-        copy.start()
-        ghosts.append(copy)
+        for part in range(HALVES):
+            base = part * half * block
+
+            def pick(i, carry):
+                for u in range(16):
+                    r = i * 16 + u
+                    picked[pl.ds(r, 1), :] = wide[pl.ds(lists[0, which, base + r], 1), :]
+                return carry
+
+            lax.fori_loop(0, half * block // 16, pick, 0)
+            rows = pl.ds(part * half, half)
+            packed[slot, rows] = picked[...].astype(jnp.bfloat16).reshape(half, block, snaps)
+            number = slot * HALVES + part
+            copy = pltpu.make_async_remote_copy(
+                src_ref=packed.at[slot, rows],
+                dst_ref=cols.at[pl.ds(own + number * half, half)],
+                send_sem=ghost_send.at[number],
+                recv_sem=ghost_recv.at[number],
+                device_id=peer,
+                device_id_type=MESH,
+            )
+            if number == 0:
+                pl.semaphore_wait(barrier, len(peers))
+            copy.start()
+            ghosts.append(copy)
 
     for load in late:
         load.wait()
@@ -177,10 +183,6 @@
         steps = own // STEP
         first, last = phase * steps // 3, (phase + 1) * steps // 3
         lax.fori_loop(first, last, one, 0)
-        rows = pl.ds(first * STEP * block, (last - first) * STEP * block)
-        store = pltpu.make_async_copy(projected.at[rows], projected_hbm.at[rows], store_sem.at[phase])
-        store.start()
-        return store
 
     for p in range(parts):
         gram[p] = total[p * height : (p + 1) * height, :]
@@ -199,23 +201,21 @@
     for d in range(1, parts):
         other, peer = in_plane(d)
         copy(0, gram.at[other], near.at[q], peer).start()
-    stores = [project(0)]
+    project(0)
     all_of(0, near).wait_recv()
     far[pl.ds(z, 1)] = jnp.sum(near[...], axis=0, keepdims=True)
     for d in sorted(range(1, depth), key=lambda d: -min(d, depth - d)):
         copy(1, far.at[z], far.at[z], along_z(d)).start()
-    stores.append(project(1))
+    project(1)
     all_of(1, far).wait_recv()
     summed[pl.ds(q, 1)] = jnp.sum(far[...], axis=0, keepdims=True)
     for d in range(1, parts):
         copy(2, summed.at[q], summed.at[q], in_plane(d)[1]).start()
-    stores.append(project(2))
+    project(2)
     all_of(2, summed).wait_recv()
     all_of(0, near).wait_send()
     all_of(1, far).wait_send()
     all_of(2, summed).wait_send()
-    for store in stores:
-        store.wait()
 
 
 def partition_terms(
@@ -233,11 +233,11 @@
     return pl.pallas_call(
         functools.partial(partition_kernel, bulk_n, group_n),
         out_shape=(
-            jax.ShapeDtypeStruct((rows, test.shape[1]), jnp.bfloat16),
-            jax.ShapeDtypeStruct((parts, height, snaps), jnp.float32),
-        ),
-        in_specs=[scalar] + [pl.BlockSpec(memory_space=pl.ANY)] * 7,
-        out_specs=(pl.BlockSpec(memory_space=pl.ANY), vmem),
+            pltpu.VMEM((rows, test.shape[1]), jnp.bfloat16),
+            pltpu.VMEM((parts, height, snaps), jnp.float32),
+        ),
+        in_specs=[scalar] + [pl.BlockSpec(memory_space=pltpu.HBM)] * 7,
+        out_specs=(vmem, vmem),
         scratch_shapes=[
             pltpu.SMEM(lists.shape, jnp.int32),
             pltpu.SMEM((entries, own), jnp.int32),
@@ -247,47 +247,45 @@
             pltpu.VMEM(test.shape, test.dtype),
             pltpu.VMEM((own + outer, block, snaps), jnp.bfloat16),
             pltpu.VMEM((rows, snaps), jnp.float32),
-            pltpu.VMEM((faces, snaps), jnp.float32),
+            pltpu.VMEM((faces // HALVES, snaps), jnp.float32),
             pltpu.VMEM((4, faces // block, block, snaps), jnp.bfloat16),
             pltpu.VMEM((kinds, block, 2 * block), jnp.float32),
             pltpu.VMEM((own, block, entries * block), jnp.bfloat16),
             pltpu.VMEM((own, block, snaps), jnp.bfloat16),
-            pltpu.VMEM((rows, test.shape[1]), jnp.bfloat16),
             pltpu.VMEM((snaps, snaps), jnp.float32),
             pltpu.VMEM((parts, height, snaps), jnp.float32),
             pltpu.VMEM((parts, height, snaps), jnp.float32),
             pltpu.VMEM((depth, height, snaps), jnp.float32),
             pltpu.SemaphoreType.DMA((CHUNKS + 1,)),
             pltpu.SemaphoreType.DMA((5,)),
-            pltpu.SemaphoreType.DMA((4,)),
-            pltpu.SemaphoreType.DMA((4,)),
-            pltpu.SemaphoreType.DMA((3,)),
+            pltpu.SemaphoreType.DMA((4 * HALVES,)),
+            pltpu.SemaphoreType.DMA((4 * HALVES,)),
             pltpu.SemaphoreType.DMA((3,)),
             pltpu.SemaphoreType.DMA((3,)),
         ],
         compiler_params=pltpu.CompilerParams(
-            collective_id=0, has_side_effects=True, vmem_limit_bytes=GRANT
+            collective_id=0, has_side_effects=True, vmem_limit_bytes=GRANT - ROOM
         ),
         name="partition_terms",
-    )(owned, lists, columns.T, types.T, scales.T, snapshots.reshape(own, block, snaps), table, test)
-
-
-def outputs_kernel(divisor, made, summed_hbm, test_hbm, projected, sketch_hbm, held, summed, test, full, sketch, sems, out_sems):
-    small = [
-        pltpu.make_async_copy(summed_hbm, summed, sems.at[PIECES]),
-        pltpu.make_async_copy(test_hbm, test, sems.at[PIECES + 1]),
-    ]
+    )(
+        owned,
+        *(
+            pltpu.with_memory_space_constraint(x, pltpu.HBM)
+            for x in (
+                lists, columns.T, types.T, scales.T, snapshots.reshape(own, block, snaps), table, test,
+            )
+        ),
+    )
+
+
+def outputs_kernel(divisor, made, summed, test_hbm, projected, sketch_hbm, test, full, sketch, sems):
     size = made.shape[0] // PIECES
     pieces = [pl.ds(n * size, size) for n in range(PIECES)]
-    loads = [pltpu.make_async_copy(made.at[p], held.at[p], sems.at[n]) for n, p in enumerate(pieces)]
-    stores = [pltpu.make_async_copy(held.at[p], projected.at[p], out_sems.at[n]) for n, p in enumerate(pieces)]
-    for copy in small + loads:
+    load = pltpu.make_async_copy(test_hbm, test, sems.at[PIECES])
+    stores = [pltpu.make_async_copy(made.at[p], projected.at[p], sems.at[n]) for n, p in enumerate(pieces)]
+    for copy in [load] + stores:
         copy.start()
-    for load, store in zip(loads, stores):
-        load.wait()
-        store.start()
-    for copy in small:
-        copy.wait()
+    load.wait()
     parts, height, _ = summed.shape
     for p in range(parts):
         full[p * height : (p + 1) * height, :] = summed[p]
@@ -296,7 +294,7 @@
         precision=lax.Precision.HIGHEST, preferred_element_type=jnp.float32,
     )
     sketch[...] = product / divisor
-    last = pltpu.make_async_copy(sketch, sketch_hbm, sems.at[PIECES + 2])
+    last = pltpu.make_async_copy(sketch, sketch_hbm, sems.at[PIECES + 1])
     last.start()
     for copy in stores + [last]:
         copy.wait()
@@ -305,27 +303,25 @@
 def final_outputs(made, summed, test):
     rows, width = made.shape
     snaps = test.shape[0]
-    anywhere = pl.BlockSpec(memory_space=pl.ANY)
+    anywhere = pl.BlockSpec(memory_space=pltpu.HBM)
+    vmem = pl.BlockSpec(memory_space=pltpu.VMEM)
     return pl.pallas_call(
         functools.partial(outputs_kernel, rows),
         out_shape=(
             jax.ShapeDtypeStruct((rows, width), jnp.bfloat16),
             jax.ShapeDtypeStruct((snaps, width), jnp.float32),
         ),
-        in_specs=[anywhere] * 3,
+        in_specs=[vmem, vmem, anywhere],
         out_specs=(anywhere, anywhere),
         scratch_shapes=[
-            pltpu.VMEM(made.shape, made.dtype),
-            pltpu.VMEM(summed.shape, jnp.float32),
             pltpu.VMEM(test.shape, jnp.bfloat16),
             pltpu.VMEM((snaps, snaps), jnp.float32),
             pltpu.VMEM((snaps, width), jnp.float32),
-            pltpu.SemaphoreType.DMA((PIECES + 3,)),
-            pltpu.SemaphoreType.DMA((PIECES,)),
+            pltpu.SemaphoreType.DMA((PIECES + 2,)),
         ],
-        compiler_params=pltpu.CompilerParams(vmem_limit_bytes=GRANT),
+        compiler_params=pltpu.CompilerParams(vmem_limit_bytes=GRANT - ROOM),
         name="final_outputs",
-    )(made, summed, test)
+    )(made, summed, pltpu.with_memory_space_constraint(test, pltpu.HBM))
 
 
 def on_device(

time: 53 us -> 50.2 us (0.947)
  Pallas kernels: 51.5 us -> 48.7 us
    pallas_call x1, Pallas kernels: 48.5 us -> 46.8 us  [partition_terms(): pl.pallas_call(functools.partial(partition_kernel, bulk_n, group_n), out_...]
    pallas_call x1, Pallas kernels: 3.04 us -> 1.9 us  [final_outputs(): pl.pallas_call(functools.partial(outputs_kernel, rows), out_shape=(jax.Sh...]
where the time goes in v4:
time: 50.2 us; the launch traced here: 50 us
  Pallas kernels  48.7 us (97%)
  between operations  1.28 us (3%)
    pallas_call x1, Pallas kernels, partition_terms(): pl.pallas_call(functools.partial(partition_kernel, bulk_n, group_n), out_...  46.8 us
    pallas_call x1, Pallas kernels, final_outputs(): pl.pallas_call(functools.partial(outputs_kernel, rows), out_shape=(jax.Sh...  1.9 us

profile of v4, /device:TPU:1, one launch (start us, length us, event | category | flops | bytes accessed | tf_op | source)
XLA Modules:
  0.0 50.0 jit_solution(12052482387618387332)
XLA Ops:
  1.3 46.8 %partition_terms.1 = (bf16[6144,256]{1,0:T(8,128)(2,1)S(1)}, f32[32,4,128]{2,1,0:T(4,128)S(1)}) custom-call(s32[1]{0:T(128)S(6)} %copy.10.owned, s32[1,4,512]{2,1,0:T(4,128)} %lists_hbm.1, s32[9,96]{1,0:T(8,128)} %bitcast.5, s32[9,96]{1,0:T(8,128)} %bitcast.6, f32[9,96]{1,0:T(8,128)} %bitcast.7, bf16[96,64,128]{2,1,0:T(8,128)(2,1)} %bitcast.4, ...), custom_call_target="tpu_custom_call" | custom-call | tf_op jit(solution)/shard_map/partition_terms/pallas_call | solution.py:233
  48.1 1.9 %final_outputs.1 = (bf16[6144,256]{1,0:T(8,128)(2,1)}, f32[128,256]{1,0:T(8,128)}) custom-call(bf16[6144,256]{1,0:T(8,128)(2,1)S(1)} %get-tuple-element.4.made, f32[32,4,128]{2,1,0:T(4,128)S(1)} %get-tuple-element.5.summed, bf16[128,256]{1,0:T(8,128)(2,1)} %test_hbm.3), custom_call_target="tpu_custom_call" | custom-call | tf_op jit(solution)/shard_map/final_outputs/pallas_call | solution.py:308

commit v5 on v4

--- a/solution.py
+++ b/solution.py
@@ -15,7 +15,7 @@
 CHUNKS = 4
 HALVES = 2
 STEP = 16
-WIDE = 4
+WIDE = 8
 
 
 def wrapped(index, count):
@@ -96,12 +96,12 @@
             base = part * half * block
 
             def pick(i, carry):
-                for u in range(16):
-                    r = i * 16 + u
+                for u in range(32):
+                    r = i * 32 + u
                     picked[pl.ds(r, 1), :] = wide[pl.ds(lists[0, which, base + r], 1), :]
                 return carry
 
-            lax.fori_loop(0, half * block // 16, pick, 0)
+            lax.fori_loop(0, half * block // 32, pick, 0)
             rows = pl.ds(part * half, half)
             packed[slot, rows] = picked[...].astype(jnp.bfloat16).reshape(half, block, snaps)
             number = slot * HALVES + part

time: 50.2 us -> 50.2 us (level)
  no operation moved by 1% of the time
where the time goes in v5:
time: 50.2 us; the launch traced here: 50 us
  Pallas kernels  48.7 us (97%)
  between operations  1.28 us (3%)
    pallas_call x1, Pallas kernels, partition_terms(): pl.pallas_call(functools.partial(partition_kernel, bulk_n, group_n), out_...  46.8 us
    pallas_call x1, Pallas kernels, final_outputs(): pl.pallas_call(functools.partial(outputs_kernel, rows), out_shape=(jax.Sh...  1.9 us

profile of v5, /device:TPU:1, one launch (start us, length us, event | category | flops | bytes accessed | tf_op | source)
XLA Modules:
  0.0 50.0 jit_solution(3476126398917349503)
XLA Ops:
  1.3 46.8 %partition_terms.1 = (bf16[6144,256]{1,0:T(8,128)(2,1)S(1)}, f32[32,4,128]{2,1,0:T(4,128)S(1)}) custom-call(s32[1]{0:T(128)S(6)} %copy.10.owned, s32[1,4,512]{2,1,0:T(4,128)} %lists_hbm.1, s32[9,96]{1,0:T(8,128)} %bitcast.5, s32[9,96]{1,0:T(8,128)} %bitcast.6, f32[9,96]{1,0:T(8,128)} %bitcast.7, bf16[96,64,128]{2,1,0:T(8,128)(2,1)} %bitcast.4, ...), custom_call_target="tpu_custom_call" | custom-call | tf_op jit(solution)/shard_map/partition_terms/pallas_call | solution.py:233
  48.1 1.9 %final_outputs.1 = (bf16[6144,256]{1,0:T(8,128)(2,1)}, f32[128,256]{1,0:T(8,128)}) custom-call(bf16[6144,256]{1,0:T(8,128)(2,1)S(1)} %get-tuple-element.4.made, f32[32,4,128]{2,1,0:T(4,128)S(1)} %get-tuple-element.5.summed, bf16[128,256]{1,0:T(8,128)(2,1)} %test_hbm.3), custom_call_target="tpu_custom_call" | custom-call | tf_op jit(solution)/shard_map/final_outputs/pallas_call | solution.py:308
